TPU v7x, 256 devices: a whole 4x4x8 slice. The times are simulated.
256 devices in a mesh: blk: 32 (over z, y_hi, core), head: 8 (over x, y_lo).
Axes of the slice: x: 4, y: 4 (y_hi: 2, y_lo: 2; y = y_hi * 2 + y_lo), z: 8, core: 2. Of those that a mesh axis runs over, the one named last changes fastest.
Arguments:
- frames: bfloat16 [32768, 2048], P(('blk', 'head')), may hold values from -20.4 to 20.4
- qkv_weight: bfloat16 [2048, 6144], P(None, 'head'), may hold values from -0.125 to 0.125
- out_weight: bfloat16 [2048, 2048], P('head'), may hold values from -0.125 to 0.125
- recording: int32 [32768], P(('blk', 'head')), may hold values from 0 to 63, never falling along the last dimension, each value on 1 to 1024 neighbouring positions
Outputs:
- encoded: bfloat16 [32768, 2048], P(('blk', 'head'))
Inputs may be any that keep to these rules, and one draw needn't show every extreme that they name: Recording ids never fall along the frames; each recording holds 1 to 1024 frames, and one holds exactly 1024.
All inputs are finite; a program needn't handle non-finite values.
Results may differ from a plain program's by a relative error of at most 0.019.
The roundings to bfloat16 on the way count: a program that leaves them out, or rounds other values in their place, can miss the bound.
Values may be sent and summed in bfloat16 or wider, within the bound.
A program may use at most 64 MiB of HBM per device.

v0:
```python
import jax
import jax.numpy as jnp
from jax import lax
from jax.sharding import PartitionSpec as P

HEAD_DIM = 128


def shifted(value, axis, by):
    peers = lax.axis_size(axis)
    pairs = [(i, i + by) for i in range(peers) if 0 <= i + by < peers]
    return lax.ppermute(value, axis, pairs)


def attend(carry, query, block, query_ids, key_ids, valid):
    maxima, totals, sums = carry
    heads = query.shape[1]
    mask = (query_ids[:, None] == key_ids[None, :]) & valid
    new_max = []
    new_tot = []
    new_sum = []
    for head in range(heads):
        keys = block[:, head, 0, :]
        values = block[:, head, 1, :]
        scores = jnp.einsum(
            "qd,kd->qk", query[:, head, :], keys, preferred_element_type=jnp.float32
        )
        scores = scores * HEAD_DIM ** (-0.5)
        scores = jnp.where(mask, scores, -jnp.inf)
        top = jnp.maximum(maxima[head], jnp.max(scores, axis=1))
        decay = jnp.exp(maxima[head] - top)
        weights = jnp.exp(scores - top[:, None])
        new_tot.append(totals[head] * decay + jnp.sum(weights, axis=1))
        product = jnp.dot(weights.astype(jnp.bfloat16), values, preferred_element_type=jnp.float32)
        new_sum.append(sums[head] * decay[:, None] + product)
        new_max.append(top)
    return (jnp.stack(new_max), jnp.stack(new_tot), jnp.stack(new_sum))


def shards(frames, qkv_weight, out_weight, recording):
    query_ids = lax.all_gather(recording, "head", axis=0, tiled=True)
    group_index = lax.axis_index("blk")
    num_groups = lax.axis_size("blk")
    qkv = jnp.dot(
        lax.all_gather(frames, "head", axis=0, tiled=True),
        qkv_weight,
        preferred_element_type=jnp.float32,
    ).astype(jnp.bfloat16)
    group = qkv.shape[0]
    heads = qkv_weight.shape[1] // (3 * HEAD_DIM)
    qkv = qkv.reshape(group, heads, 3, HEAD_DIM)
    query = qkv[:, :, 0, :]
    own_kv = qkv[:, :, 1:, :]
    carry = (
        jnp.full((heads, group), -jnp.inf, jnp.float32),
        jnp.zeros((heads, group), jnp.float32),
        jnp.zeros((heads, group, HEAD_DIM), jnp.float32),
    )
    carry = attend(carry, query, own_kv, query_ids, query_ids, True)

    def visit(carry, block, key_ids, source):
        valid = (source >= 0) & (source < num_groups)
        return attend(carry, query, block, query_ids, key_ids, valid)

    lower = own_kv
    lower_ids = query_ids
    upper = own_kv
    upper_ids = query_ids
    lower, lower_ids = shifted((lower, lower_ids), "blk", 1)
    upper, upper_ids = shifted((upper, upper_ids), "blk", -1)
    carry = visit(carry, lower, lower_ids, group_index - 1)
    carry = visit(carry, upper, upper_ids, group_index + 1)
    maxima, totals, sums = carry
    mixed = (sums / totals[:, :, None]).astype(jnp.bfloat16)
    attended = jnp.transpose(mixed, (1, 0, 2)).reshape(group, heads * HEAD_DIM)
    return lax.psum_scatter(
        jnp.dot(attended, out_weight, preferred_element_type=jnp.float32).astype(jnp.bfloat16),
        "head",
        scatter_dimension=0,
        tiled=True,
    )


def solution(mesh):
    in_specs = (P(("blk", "head"), None), P(None, "head"), P("head", None), P(("blk", "head")))
    out_specs = P(("blk", "head"), None)
    return jax.shard_map(shards, mesh=mesh, in_specs=in_specs, out_specs=out_specs, check_vma=False)
```

profile of v0, /device:TPU:1, one launch (start us, length us, event | category | flops | bytes accessed | tf_op | source)
XLA Modules:
  0.0 287.6 jit_solution(7080596217212093793)
XLA Ops:
  6.5 0.7 all-gather.3.cloned.1.call-update
  7.3 0.0 reduce-scatter.2.cloned.1.call-start
  7.3 98.0 %all-gather.3.cloned.1.call-done = bf16[1024,2048]{1,0:T(8,128)(2,1)} async-done(((bf16[128,2048]{1,0:T(8,128)(2,1)}), bf16[1024,2048]{1,0:T(8,128)(2,1)}) %all-gather.3.cloned.1.call-update) | async-done | bytes 4194320 | tf_op jit(solution)/shard_map/all_gather | solution.py:45
  105.3 5.7 %convolution_convert_fusion.1 = bf16[1024,768]{0,1:T(8,128)(2,1)S(1)} fusion(bf16[1024,2048]{1,0:T(8,128)(2,1)} %all-gather.3.cloned.1.call-done, bf16[2048,768]{1,0:T(8,128)(2,1)S(1)} %copy-done), kind=kOutput, calls=%fused_computation.41 | convolution fusion | flops 3222011904 | bytes 8912896 | tf_op jit(solution)/shard_map/dot_general | solution.py:44
  110.9 1.1 copy-done.1
  112.1 1.0 slice.76
  113.1 5.0 %collective-permute-start.1 = (bf16[1024,2,2,128]{0,3,2,1:T(8,128)(2,1)}, bf16[1024,2,2,128]{0,3,2,1:T(8,128)(2,1)}, u32[]{:S(2)}, u32[]{:S(2)}) collective-permute-start(bf16[1024,2,2,128]{0,3,2,1:T(8,128)(2,1)} %slice.76), channel_id=1, source_target_pairs={{0,8},{8,16},{16,24},{24,32},{32,40},{40,48},{48,56},{56,64},{64,7... | collective-permute-start | bytes 3145736 | tf_op jit(solution)/shard_map/ppermute | solution.py:12
  118.1 23.2 %all-gather = s32[8,1,128]{2,1,0:T(1,128)S(1)} all-gather(s32[1,1,128]{2,1,0:T(1,128)S(1)} %bitcast.117), channel_id=1, replica_groups=mesh['blk'=32,'head'=8] {'head'}, dimensions={0}, use_global_device_ids=true | all-gather | bytes 4608 | tf_op jit(solution)/shard_map/all_gather | solution.py:41
  141.3 1.9 collective-permute-start.2
  143.2 5.1 %collective-permute-start = (s32[1024]{0:T(1024)S(1)}, s32[1024]{0:T(1024)S(1)}, u32[]{:S(2)}, u32[]{:S(2)}) collective-permute-start(s32[1024]{0:T(1024)S(1)} %bitcast.101), channel_id=1, source_target_pairs={{0,8},{8,16},{16,24},{24,32},{32,40},{40,48},{48,56},{56,64},{64,7... | collective-permute-start | bytes 12296 | tf_op jit(solution)/shard_map/ppermute | solution.py:12
  148.4 2.2 collective-permute-start.3
  150.7 1.1 slice_bitcast_fusion
  151.7 1.7 fusion.65
  153.5 0.7 fusion.68
  154.2 0.0 collective-permute-done
  154.2 2.8 fusion.14
  157.1 1.3 fusion.38
  158.4 1.7 fusion.64
  160.1 6.3 %collective-permute-done.3 = bf16[1024,2,2,128]{0,3,2,1:T(8,128)(2,1)S(1)} collective-permute-done((bf16[1024,2,2,128]{0,3,2,1:T(8,128)(2,1)}, bf16[1024,2,2,128]{0,3,2,1:T(8,128)(2,1)S(1)}, u32[]{:S(2)}, u32[]{:S(2)}) %collective-permute-start.3) | collective-permute-done | bytes 1048608 | tf_op jit(solution)/shard_map/ppermute | solution.py:12
  166.4 5.2 %fusion = (f32[1024]{0:T(1024)S(1)}, f32[1024]{0:T(1024)S(1)}, f32[1024]{0:T(1024)S(1)}, f32[1024]{0:T(1024)S(1)}, f32[1024]{0:T(1024)S(1)}, /*index=5*/f32[1024,1024]{0,1:T(8,128)S(1)}) fusion(f32[1024,1024]{0,1:T(8,128)S(1)} %fusion.68, f32[1024]{0:T(1024)S(1)} %get-tuple-element.17, s32[1024]{0:T(1024)S(1)} %bitcast.104, pred[]{:T(512)S(6)} %and.22, ...), kind=kOutput, calls=%fused_computation.15 | convolution fusion | flops 291499008 | bytes 21540866 | tf_op jit(solution)/shard_map/qd,kd->qk/dot_general | solution.py:25
  171.6 1.2 fusion.41
  172.8 4.9 %fusion.4 = (f32[1024]{0:T(1024)S(1)}, f32[1024]{0:T(1024)S(1)}, f32[1024]{0:T(1024)S(1)}, f32[1024]{0:T(1024)S(1)}, f32[1024,1024]{0,1:T(8,128)S(1)}) fusion(f32[1024,1024]{0,1:T(8,128)S(1)} %get-tuple-element.29, f32[1024]{0:T(1024)S(1)} %get-tuple-element.32, s32[1024]{0:T(1024)S(1)} %bitcast.106, s32[1024]{0:T(1024)S(1)} %collective-permute-done.2, ...), kind=kOutput, calls=%fused_computation.19 | convolution fusion | flops 289402880 | bytes 17346562 | tf_op jit(solution)/shard_map/qd,kd->qk/dot_general | solution.py:25
  177.7 1.8 fusion.10
  179.5 1.6 fusion.28
  181.2 1.6 fusion.24
  182.8 2.6 fusion.59
  185.4 0.0 copy-start.3
  185.4 2.7 fusion.50
  188.1 0.1 fusion.62
  188.2 3.2 %convolution_convert_fusion = bf16[1024,2048]{1,0:T(8,128)(2,1)} fusion(bf16[1024,256]{0,1:T(8,128)(2,1)S(1)} %bitcast.86, bf16[256,2048]{1,0:T(8,128)(2,1)S(1)} %copy-done.3), kind=kOutput, calls=%fused_computation.14 | convolution fusion | flops 1075838976 | bytes 5767168 | tf_op jit(solution)/shard_map/dot_general | solution.py:77
  191.5 0.0 reduce-scatter.2.cloned.1.call-update
  191.5 89.3 %reduce-scatter.2.cloned.1.call-done = bf16[128,2048]{1,0:T(8,128)(2,1)} async-done(((bf16[1024,2048]{1,0:T(8,128)(2,1)}), bf16[128,2048]{1,0:T(8,128)(2,1)}) %reduce-scatter.2.cloned.1.call-update) | async-done | bytes 524304 | tf_op jit(solution)/shard_map/reduce_scatter | solution.py:76
  (17 shorter events, 0.1 us)
Async XLA Ops:
  6.5 98.7 %copy-start = (bf16[2048,768]{1,0:T(8,128)(2,1)S(1)}, bf16[2048,768]{1,0:T(8,128)(2,1)}, u32[]{:S(2)}) copy-start(bf16[2048,768]{1,0:T(8,128)(2,1)} %param.5) | copy-start | bytes 9437188
  6.5 98.7 %all-gather.3.cloned.1.call-start = ((), (), s32[]{:S(2)}) async-start(), calls=%async_computation.1 | async-start | bytes 4718592 | tf_op jit(solution)/shard_map/all_gather | solution.py:45
  7.3 110.9 %copy-start.4 = (s32[128]{0:T(128)S(1)}, s32[128]{0:T(128)}, u32[]{:S(2)}) copy-start(s32[128]{0:T(128)} %param.7) | copy-start | bytes 1540
  7.3 273.5 %reduce-scatter.2.cloned.1.call-start = ((), (), s32[]{:S(2)}) async-start(), calls=%async_computation.2 | async-start | bytes 4718592 | tf_op jit(solution)/shard_map/reduce_scatter | solution.py:76
  110.9 1.2 copy-start.1
  113.1 41.1 %collective-permute-start.1 = (bf16[1024,2,2,128]{0,3,2,1:T(8,128)(2,1)}, bf16[1024,2,2,128]{0,3,2,1:T(8,128)(2,1)}, u32[]{:S(2)}, u32[]{:S(2)}) collective-permute-start(bf16[1024,2,2,128]{0,3,2,1:T(8,128)(2,1)} %slice.76), channel_id=1, source_target_pairs={{0,8},{8,16},{16,24},{24,32},{32,40},{40,48},{48,56},{56,64},{64,7... | collective-permute-start | bytes 3145736 | tf_op jit(solution)/shard_map/ppermute | solution.py:12
  141.3 18.7 %collective-permute-start.2 = (s32[1024]{0:T(1024)S(1)}, s32[1024]{0:T(1024)S(1)}, u32[]{:S(2)}, u32[]{:S(2)}) collective-permute-start(s32[1024]{0:T(1024)S(1)} %bitcast.100), channel_id=1, source_target_pairs={{8,0},{16,8},{24,16},{32,24},{40,32},{48,40},{56,48},{64,56},{72,6... | collective-permute-start | bytes 12296 | tf_op jit(solution)/shard_map/ppermute | solution.py:12
  143.2 11.0 %collective-permute-start = (s32[1024]{0:T(1024)S(1)}, s32[1024]{0:T(1024)S(1)}, u32[]{:S(2)}, u32[]{:S(2)}) collective-permute-start(s32[1024]{0:T(1024)S(1)} %bitcast.101), channel_id=1, source_target_pairs={{0,8},{8,16},{16,24},{24,32},{32,40},{40,48},{48,56},{56,64},{64,7... | collective-permute-start | bytes 12296 | tf_op jit(solution)/shard_map/ppermute | solution.py:12
  148.4 5.0 %copy-start.2 = (bf16[1024,768]{0,1:T(8,128)(2,1)S(1)}, bf16[1024,768]{0,1:T(8,128)(2,1)}, u32[]{:S(2)}) copy-start(bf16[1024,768]{0,1:T(8,128)(2,1)} %copy-done.1) | copy-start | bytes 4718596
  148.4 18.0 %collective-permute-start.3 = (bf16[1024,2,2,128]{0,3,2,1:T(8,128)(2,1)}, bf16[1024,2,2,128]{0,3,2,1:T(8,128)(2,1)S(1)}, u32[]{:S(2)}, u32[]{:S(2)}) collective-permute-start(bf16[1024,2,2,128]{0,3,2,1:T(8,128)(2,1)} %slice.76), channel_id=1, source_target_pairs={{8,0},{16,8},{24,16},{32,24},{40,32},{48,40},{56,48},{64,56},{72,6... | collective-permute-start | bytes 3145736 | tf_op jit(solution)/shard_map/ppermute | solution.py:12
  185.4 2.8 copy-start.3
Sparse Core Ops, SparseCore 0:
  9.1 96.0 all-gather.2
  191.6 89.1 reduce-scatter.1
where the time goes:
time: 288 us
  waiting for transfers between devices  194 us (67%)
  matrix products  36.9 us (13%)
  blocking collectives  23.2 us (8%)
  starting transfers between devices  14.3 us (5%)
  between operations  13.7 us (5%)
  local copies, waits for them, and re-layouts  3.28 us (1%)
    all_gather x1, waiting for transfers between devices, shards(): lax.all_gather(frames, 'head', axis=0, tiled=True)  98 us
    reduce_scatter x1, waiting for transfers between devices, shards(): lax.psum_scatter(jnp.dot(attended, out_weight, preferred_element_type=jnp...  89.3 us
    all_gather x1, blocking collectives, shards(): query_ids = lax.all_gather(recording, 'head', axis=0, tiled=True)  23.2 us
    dot_general x6, matrix products, attend(): jnp.einsum('qd,kd->qk', query[:, head, :], keys, preferred_element_type=j...  17 us
    ppermute x4, starting transfers between devices, shifted(): return lax.ppermute(value, axis, pairs)  14.3 us
    dot_general x6, matrix products, attend(): jnp.dot(weights.astype(jnp.bfloat16), values, preferred_element_type=jnp....  11 us
    ppermute x4, waiting for transfers between devices, shifted(): return lax.ppermute(value, axis, pairs)  6.32 us
  transfers between devices with their start and end apart: 6, of which 3 were waited for; matrix products, arithmetic and copies ran while one was open for 3% of the time, Pallas kernels for 0%

commit v1 on v0

v1 whole, which is shorter than its diff:
```python
import functools

import jax
import jax.numpy as jnp
from jax import lax
from jax.experimental import pallas as pl
from jax.experimental.pallas import tpu as pltpu
from jax.sharding import PartitionSpec as P

HEAD_DIM = 128
MESH = pl.DeviceIdType.MESH
NX, NZ, NB = 4, 8, 32
BF = jnp.bfloat16
F32 = jnp.float32
NEG = -jnp.inf


def mod(a, n):
    return lax.rem(a + 2 * n, n)


def kernel(
    frames, qw_in, ow, ids, out,
    F, QW, W, Q, KV, H, RL, IDS, HID, RID, QID, ATS, ATR, ACC, M, L, A,
    loc, ag_s, ag_r, id_s, id_r, hid_s, hid_r, sib_s, sib_r, off_s, off_r, rel_s, rel_r,
    wp_s, wp_r, wu_s, wu_r, wd_s, wd_r, ws_s, ws_r, at_s, at_r,
):
    blk = lax.axis_index("blk")
    head = lax.axis_index("head")
    z = blk // 4
    yh = lax.rem(blk, 4) // 2
    c = lax.rem(blk, 2)
    x = head // 2
    yl = lax.rem(head, 2)

    def block(dx, f):
        return mod(x + dx, NX) * 2 + lax.rem(yl + f, 2)

    def peer(dx, f):
        return (blk, block(dx, f))

    right, left, across = peer(1, 0), peer(-1, 0), peer(0, 1)
    sibling = (blk + 1 - 2 * c, head)
    above = (mod(blk + 4, NB), head)
    below = (mod(blk - 4, NB), head)
    owner_blk = z * 4 + (1 - yh) * 2 + c
    owner_head = x * 2 + 1 - yl
    relay = (owner_blk, owner_head)
    relay_to = (mod(owner_blk + 2 * c - 1, NB), owner_head)
    far = mod(blk + 2 * c - 1, NB)
    relay_from = ((far // 4) * 4 + (1 - lax.rem(far, 4) // 2) * 2 + lax.rem(far, 2), owner_head)
    base_off = 8 * (1 - c)
    base_sib = 8 * c

    def remote(src, dst, ss, rs, dev):
        return pltpu.make_async_remote_copy(
            src_ref=src, dst_ref=dst, send_sem=ss, recv_sem=rs, device_id=dev, device_id_type=MESH
        )

    load_qw = pltpu.make_async_copy(qw_in, QW, loc.at[0])
    load_own = pltpu.make_async_copy(frames, F.at[head], loc.at[1])
    load_w = pltpu.make_async_copy(ow, W.at[0], loc.at[2])
    load_own.start()
    load_qw.start()
    load_w.start()
    rels = [(dx, f) for dx in range(NX) for f in range(2)]
    partners = [peer(dx, f) for dx, f in rels[1:]]
    partners += [sibling, above, below, relay, relay_to, relay_from]
    barrier = pltpu.get_barrier_semaphore()
    for p in partners:
        pl.semaphore_signal(barrier, inc=1, device_id=p, device_id_type=MESH)
    pl.semaphore_wait(barrier, len(partners))

    piece = [None]
    for k in range(1, 8):
        dx, f = rels[k]
        back = ((-dx) % NX) * 2 + f
        piece.append(remote(ow.at[z, c], W.at[back, z, c], wp_s.at[k], wp_r.at[back], peer(dx, f)))
    for k in (1, 2, 6, 3, 7, 4, 5):
        piece[k].start()

    def fr(dx, f, half=None):
        ref = F.at[block(dx, f)]
        if half is None:
            return ref
        return ref.at[pl.ds(64 * half, 64)]

    def gather_copy(i, src, dst, dev):
        return remote(src, dst, ag_s.at[i], ag_r.at[i], dev)

    send = [
        gather_copy(0, frames, fr(0, 0), right),
        gather_copy(1, frames, fr(0, 0), left),
        gather_copy(2, frames, fr(0, 0), across),
        gather_copy(3, fr(-1, 0, 0), fr(-1, 0, 0), right),
        gather_copy(4, fr(1, 0, 1), fr(1, 0, 1), left),
        gather_copy(5, fr(0, 1), fr(0, 1), right),
        gather_copy(6, fr(0, 1), fr(0, 1), left),
        gather_copy(7, fr(-1, 1, 0), fr(-1, 1, 0), right),
        gather_copy(8, fr(1, 1, 1), fr(1, 1, 1), left),
    ]
    recv = [
        gather_copy(0, fr(-1, 0), fr(-1, 0), right),
        gather_copy(1, fr(1, 0), fr(1, 0), right),
        gather_copy(2, fr(0, 1), fr(0, 1), right),
        gather_copy(3, fr(2, 0, 0), fr(2, 0, 0), right),
        gather_copy(4, fr(2, 0, 1), fr(2, 0, 1), right),
        gather_copy(5, fr(-1, 1), fr(-1, 1), right),
        gather_copy(6, fr(1, 1), fr(1, 1), right),
        gather_copy(7, fr(2, 1, 0), fr(2, 1, 0), right),
        gather_copy(8, fr(2, 1, 1), fr(2, 1, 1), right),
    ]
    send[0].start()
    send[1].start()
    send[2].start()

    idc = [None]
    for k in range(1, 8):
        dx, f = rels[k]
        back = ((-dx) % NX) * 2 + f
        idc.append(remote(ids, IDS.at[head], id_s.at[k], id_r.at[back], peer(dx, f)))
        idc[k].start()
    IDS[head] = ids[...]

    def kv_copies(b):
        return (
            remote(KV.at[b], H.at[base_sib + b], sib_s.at[b], sib_r.at[b], sibling),
            remote(KV.at[b], RL.at[b], off_s.at[b], off_r.at[b], relay),
        )

    def relay_copy(b):
        return remote(RL.at[b], H.at[base_off + b], rel_s.at[b], rel_r.at[b], relay_to)

    def project(b):
        r = jnp.dot(F[b], QW[...], preferred_element_type=F32).astype(BF)
        for hd in range(2):
            o = hd * 3 * HEAD_DIM
            cols = pl.ds(hd * HEAD_DIM, HEAD_DIM)
            Q[b, :, cols] = r[:, o : o + HEAD_DIM]
            KV[b, 0, :, cols] = r[:, o + HEAD_DIM : o + 2 * HEAD_DIM]
            KV[b, 1, :, cols] = r[:, o + 2 * HEAD_DIM : o + 3 * HEAD_DIM]
        to_sib, to_off = kv_copies(b)
        to_off.start()
        to_sib.start()

    def pass_on(dx, f):
        b = mod(x + dx, NX) * 2 + lax.rem(1 - yl + f, 2)
        remote(RL.at[b], RL.at[b], off_s.at[b], off_r.at[b], relay).wait_recv()
        relay_copy(b).start()

    def wz(s, up):
        return mod(z - s, NZ) if up else mod(z + s, NZ)

    def w_set(zs, part):
        return W.at[pl.ds(*part), zs, c]

    FULL, UPART, DPART = (1, 7), (1, 4), (5, 3)

    def w_send(s, up):
        zs = wz(s - 1, up)
        part = FULL if s < 4 else (UPART if up else DPART)
        ref = w_set(zs, part)
        if up:
            return remote(ref, ref, wu_s.at[s], wu_r.at[s], above)
        return remote(ref, ref, wd_s.at[s], wd_r.at[s], below)

    def w_recv(s, up):
        zs = wz(s, up)
        part = FULL if s < 4 else (UPART if up else DPART)
        ref = w_set(zs, part)
        if up:
            return remote(ref, ref, wu_s.at[s], wu_r.at[s], above)
        return remote(ref, ref, wd_s.at[s], wd_r.at[s], below)

    def w_sib(j):
        ref = w_set(mod(z + j, NZ), FULL)
        return remote(ref, ref, ws_s.at[j], ws_r.at[j], sibling)

    def w_sib_recv(j):
        ref = W.at[pl.ds(*FULL), mod(z + j, NZ), 1 - c]
        return remote(ref, ref, ws_s.at[j], ws_r.at[j], sibling)

    def w_step(s):
        w_recv(s, True).wait_recv()
        w_send(s + 1, True).start()
        w_recv(s, False).wait_recv()
        w_send(s + 1, False).start()
        w_sib(8 - s).start()
        w_sib(s).start()

    load_own.wait()
    load_qw.wait()
    project(head)

    for k in range(1, 8):
        remote(W.at[k, z, c], W.at[k, z, c], wp_s.at[k], wp_r.at[k], across).wait_recv()
    w_send(1, True).start()
    w_send(1, False).start()
    w_sib(0).start()

    for k in range(1, 8):
        dx, f = rels[k]
        row = IDS.at[block(dx, f)]
        remote(row, row, id_s.at[k], id_r.at[k], across).wait_recv()
    ids_sib = remote(IDS, HID.at[pl.ds(base_sib, 8)], hid_s.at[0], hid_r.at[0], sibling)
    ids_off = remote(IDS, RID, hid_s.at[1], hid_r.at[1], relay)
    ids_rel = remote(RID, HID.at[pl.ds(base_off, 8)], hid_s.at[2], hid_r.at[2], relay_to)
    ids_off.start()
    ids_sib.start()
    for b in range(8):
        QID[b] = jnp.transpose(jnp.broadcast_to(IDS[b], (128, 128)))

    recv[0].wait_recv()
    send[3].start()
    recv[1].wait_recv()
    send[4].start()
    recv[2].wait_recv()
    send[5].start()
    send[6].start()
    pass_on(0, 0)
    ids_off.wait_recv()
    ids_rel.start()
    project(block(0, 1))
    project(block(-1, 0))
    project(block(1, 0))
    w_step(1)
    pass_on(0, 1)
    recv[3].wait_recv()
    recv[4].wait_recv()
    project(block(2, 0))
    pass_on(-1, 0)
    pass_on(1, 0)
    pass_on(2, 0)
    recv[5].wait_recv()
    send[7].start()
    recv[6].wait_recv()
    send[8].start()
    project(block(-1, 1))
    project(block(1, 1))
    w_step(2)
    pass_on(-1, 1)
    pass_on(1, 1)
    recv[7].wait_recv()
    recv[8].wait_recv()
    project(block(2, 1))
    w_step(3)
    pass_on(2, 1)

    scale = HEAD_DIM ** (-0.5)
    dims = (((1,), (1,)), ((), ()))

    own_ids = jnp.concatenate([IDS[j] for j in range(8)], axis=1)

    def own_step(i, carry):
        qid = jnp.concatenate([QID[i]] * 8, axis=1)
        mask = qid == own_ids
        for hd in range(2):
            cols = pl.ds(hd * HEAD_DIM, HEAD_DIM)
            q = Q[i, :, cols]
            k = KV[:, 0, :, cols].reshape(1024, HEAD_DIM)
            v = KV[:, 1, :, cols].reshape(1024, HEAD_DIM)
            s = lax.dot_general(q, k, dims, preferred_element_type=F32) * scale
            s = jnp.where(mask, s, NEG)
            m = jnp.max(s, axis=1, keepdims=True)
            p = jnp.exp(s - m)
            M[i, hd] = m
            L[i, hd] = jnp.sum(p, axis=1, keepdims=True)
            A[i, hd] = jnp.dot(p.astype(BF), v, preferred_element_type=F32)
        return carry

    lax.fori_loop(0, 8, own_step, 0)

    for b in range(8):
        hs, ho = H.at[8 - base_sib + b], H.at[8 - base_off + b]
        remote(hs, hs, sib_s.at[b], sib_r.at[b], sibling).wait_recv()
        remote(ho, ho, rel_s.at[b], rel_r.at[b], sibling).wait_recv()
    hs, ho = HID.at[pl.ds(8 - base_sib, 8)], HID.at[pl.ds(8 - base_off, 8)]
    remote(hs, hs, hid_s.at[0], hid_r.at[0], sibling).wait_recv()
    remote(ho, ho, hid_s.at[2], hid_r.at[2], sibling).wait_recv()

    def halo_step(t, carry):
        d = 7 - t
        dx = d // 2
        f = lax.rem(d, 2)
        i = block(dx, f)
        kid = jnp.concatenate([HID[i + j] for j in range(9)], axis=1)
        qid = jnp.concatenate([QID[i]] * 9, axis=1)
        mask = qid == kid
        for hd in range(2):
            cols = pl.ds(hd * HEAD_DIM, HEAD_DIM)
            q = Q[i, :, cols]
            k = H[pl.ds(i, 9), 0, :, cols].reshape(9 * 128, HEAD_DIM)
            v = H[pl.ds(i, 9), 1, :, cols].reshape(9 * 128, HEAD_DIM)
            s = lax.dot_general(q, k, dims, preferred_element_type=F32) * scale
            s = jnp.where(mask, s, NEG)
            m0 = M[i, hd]
            m = jnp.maximum(m0, jnp.max(s, axis=1, keepdims=True))
            p = jnp.exp(s - m)
            decay = jnp.exp(m0 - m)
            total = L[i, hd] * decay + jnp.sum(p, axis=1, keepdims=True)
            mixed = A[i, hd] * decay + jnp.dot(p.astype(BF), v, preferred_element_type=F32)
            ATS[d, :, cols] = (mixed / total).astype(BF)
        back = mod(-dx, NX) * 2 + f

        @pl.when(d > 0)
        def _():
            remote(ATS.at[d], ATR.at[back], at_s.at[d], at_r.at[back], (blk, i)).start()

        return carry

    lax.fori_loop(0, 8, halo_step, 0)

    w_recv(4, True).wait_recv()
    w_recv(4, False).wait_recv()
    w_sib(4).start()
    load_w.wait()
    for j in range(8):
        w_sib_recv(j).wait_recv()

    def out_part(a, d):
        return jnp.dot(a, W[d].reshape(256, 2048), preferred_element_type=F32)

    ACC[...] = out_part(ATS[0], 0)

    def out_step(t, carry):
        d = 7 - t
        remote(ATR.at[d], ATR.at[d], at_s.at[d], at_r.at[d], sibling).wait_recv()
        ACC[...] += out_part(ATR[d], d)
        return carry

    lax.fori_loop(0, 7, out_step, 0)
    out[...] = ACC[...].astype(BF)

    for k in range(1, 8):
        piece[k].wait_send()
        idc[k].wait_send()
        remote(ATS.at[k], ATR.at[k], at_s.at[k], at_r.at[k], sibling).wait_send()
    for i in range(9):
        send[i].wait_send()
    for b in range(8):
        to_sib, to_off = kv_copies(b)
        to_sib.wait_send()
        to_off.wait_send()
        relay_copy(b).wait_send()
        w_sib(b).wait_send()
    ids_sib.wait_send()
    ids_off.wait_send()
    ids_rel.wait_send()
    for s in range(1, 5):
        w_send(s, True).wait_send()
        w_send(s, False).wait_send()


def shards(frames, qkv_weight, out_weight, recording):
    dma = pltpu.SemaphoreType.DMA
    any_ = pl.BlockSpec(memory_space=pl.ANY)
    vmem = pl.BlockSpec(memory_space=pltpu.VMEM)
    V = pltpu.VMEM
    return pl.pallas_call(
        kernel,
        name="encoder_block",
        out_shape=jax.ShapeDtypeStruct((128, 2048), BF),
        in_specs=[any_, any_, any_, vmem],
        out_specs=vmem,
        scratch_shapes=[
            V((8, 128, 2048), BF),
            V((2048, 768), BF),
            V((8, 8, 2, 16, 2048), BF),
            V((8, 128, 256), BF),
            V((8, 2, 128, 256), BF),
            V((16, 2, 128, 256), BF),
            V((8, 2, 128, 256), BF),
            V((8, 1, 128), jnp.int32),
            V((16, 1, 128), jnp.int32),
            V((8, 1, 128), jnp.int32),
            V((8, 128, 128), jnp.int32),
            V((8, 128, 256), BF),
            V((8, 128, 256), BF),
            V((128, 2048), F32),
            V((8, 2, 128, 1), F32),
            V((8, 2, 128, 1), F32),
            V((8, 2, 128, 128), F32),
            dma((3,)),
            dma((9,)), dma((9,)),
            dma((8,)), dma((8,)),
            dma((3,)), dma((3,)),
            dma((8,)), dma((8,)),
            dma((8,)), dma((8,)),
            dma((8,)), dma((8,)),
            dma((8,)), dma((8,)),
            dma((5,)), dma((5,)),
            dma((5,)), dma((5,)),
            dma((8,)), dma((8,)),
            dma((8,)), dma((8,)),
        ],
        compiler_params=pltpu.CompilerParams(
            collective_id=0, has_side_effects=True, vmem_limit_bytes=56 * 2**20
        ),
    )(frames, qkv_weight, out_weight.reshape(8, 2, 16, 2048), recording.reshape(1, 128))


def solution(mesh):
    in_specs = (P(("blk", "head"), None), P(None, "head"), P("head", None), P(("blk", "head")))
    out_specs = P(("blk", "head"), None)
    return jax.shard_map(shards, mesh=mesh, in_specs=in_specs, out_specs=out_specs, check_vma=False)
```

time: 288 us -> 88.1 us (0.31)
  waiting for transfers between devices: 194 us -> 0 us
  Pallas kernels: 0 us -> 85.6 us
  matrix products: 36.9 us -> 0 us
  blocking collectives: 23.2 us -> 0 us
  starting transfers between devices: 14.3 us -> 0 us
  between operations: 13.7 us -> 0.01 us
    all_gather x1 -> x0, waiting for transfers between devices: 98 us -> none  [shards(): lax.all_gather(frames, 'head', axis=0, tiled=True)]
    reduce_scatter x1 -> x0, waiting for transfers between devices: 89.3 us -> none  [shards(): lax.psum_scatter(jnp.dot(attended, out_weight, preferred_element_type=jnp...]
    pallas_call x0 -> x1, Pallas kernels: none -> 85.6 us  [shards(): pl.pallas_call(kernel, name='encoder_block', out_shape=jax.ShapeDtypeStru...]
    dot_general x14 -> x0, matrix products: 36.9 us -> none  [the longest x6 17 us: attend(): jnp.einsum('qd,kd->qk', query[:, head, :], keys, preferred_element_type=j...]
    all_gather x1 -> x0, blocking collectives: 23.2 us -> none  [shards(): query_ids = lax.all_gather(recording, 'head', axis=0, tiled=True)]
    ppermute x4 -> x0, starting transfers between devices: 14.3 us -> none  [shifted(): return lax.ppermute(value, axis, pairs)]
    ppermute x4 -> x0, waiting for transfers between devices: 6.32 us -> none  [shifted(): return lax.ppermute(value, axis, pairs)]
  transfers between devices with their start and end apart: 6 -> 0, of which waited for: 3 -> 0; matrix products, arithmetic and copies ran while one was open for 3% -> 0% of each run, Pallas kernels for 0% -> 0%
where the time goes in v1:
time: 88.1 us; the launch traced here: 87.5 us
  Pallas kernels  85.6 us (97%)
  local copies, waits for them, and re-layouts  1.88 us (2%)
    pallas_call x1, Pallas kernels, shards(): pl.pallas_call(kernel, name='encoder_block', out_shape=jax.ShapeDtypeStru...  85.6 us
    unnamed x1, local copies, waits for them, and re-layouts  1.88 us

profile of v1, /device:TPU:1, one launch (start us, length us, event | category | flops | bytes accessed | tf_op | source)
XLA Modules:
  0.0 87.5 jit_solution(13458389959061334855)
XLA Ops:
  0.0 85.6 %encoder_block.1 = bf16[128,2048]{1,0:T(8,128)(2,1)} custom-call(bf16[128,2048]{1,0:T(8,128)(2,1)} %frames.1, bf16[2048,768]{1,0:T(8,128)(2,1)} %qw_in.1, bf16[8,2,16,2048]{3,2,1,0:T(8,128)(2,1)} %bitcast.2, s32[1,128]{1,0:T(1,128)} %bitcast.3), custom_call_target="tpu_custom_call" | custom-call | tf_op jit(solution)/shard_map/encoder_block/pallas_call | solution.py:359
  85.7 1.9 %copy.6 = bf16[128,2048]{1,0:T(8,128)(2,1)} copy(bf16[128,2048]{1,0:T(8,128)(2,1)} %encoder_block.1) | data formatting | bytes 1048576
